TPU v7x, 512 devices: a whole 4x4x16 slice. The times are simulated.
512 devices in a mesh: ctx: 64 (over x, z_hi, y, core), head: 8 (over z_lo).
Axes of the slice: x: 4, y: 4, z: 16 (z_hi: 2, z_lo: 8; z = z_hi * 8 + z_lo), core: 2. Of those that a mesh axis runs over, the one named last changes fastest.
Arguments:
- queries: bfloat16 [64, 2, 512, 1024], P('ctx', None, None, 'head'), may hold values from -8 to 8
- key_states: bfloat16 [64, 2, 512, 128], P('ctx', None, 'head'), may hold values from -6 to 6
- value_states: bfloat16 [64, 2, 512, 128], P('ctx', None, 'head'), may hold values from -6 to 6
- out_grad: bfloat16 [64, 2, 512, 1024], P('ctx', None, None, 'head'), may hold values from -6 to 6
- segments: int32 [65536], replicated, may hold values from 0 to 169, never falling along the last dimension, each value on 1 to 1536 neighbouring positions
Outputs:
- attended: bfloat16 [64, 2, 512, 1024], P('ctx', None, None, 'head')
- query_grad: bfloat16 [64, 2, 512, 1024], P('ctx', None, None, 'head')
- key_grad: bfloat16 [64, 2, 512, 128], P('ctx', None, 'head')
- value_grad: bfloat16 [64, 2, 512, 128], P('ctx', None, 'head')
Inputs may be any that keep to these rules, and one draw needn't show every extreme that they name: `segments`: document numbers never fall along the sequence; every document covers at most 1536 positions, and one covers exactly that many.
All inputs are finite; a program needn't handle non-finite values.
Results may differ from a plain program's by a relative error of at most 0.017.
Values may be sent and summed in bfloat16 or wider, within the bound.
No kernel may reach another device: no remote copies, remote signals or barrier semaphores. Data moves between devices by JAX's collectives and lax.ppermute only.
A program may use at most 64 MiB of HBM per device.

v0:
```python
import jax
import jax.numpy as jnp
from jax import lax
from jax.sharding import PartitionSpec as P

REACH = 3
NEG_FILL = -1e30


def shifted(array, axis, by):
    peers = lax.axis_size(axis)
    pairs = [(i, i + by) for i in range(peers) if 0 <= i + by < peers]
    return lax.ppermute(array, axis, pairs)


def advance_whole(lower, upper, last_device):
    moved_lower = shifted(lower, "ctx", 1)
    moved_upper = shifted(upper, "ctx", -1)
    return (moved_lower, jnp.where(last_device, lower, moved_upper))


def retreat_whole(stacked, last_device):
    moved_lower = shifted(stacked[0], "ctx", -1)
    moved_upper = shifted(stacked[1], "ctx", 1)
    return jnp.stack([jnp.where(last_device, stacked[1], moved_lower), moved_upper])


def tile_allowed(segments, query_block, key_block, width):
    query_seg = lax.dynamic_slice_in_dim(segments, query_block * width, width)
    key_seg = lax.dynamic_slice_in_dim(segments, jnp.maximum(key_block, 0) * width, width)
    offsets = jnp.arange(width, dtype=jnp.int32)
    query_pos = query_block * width + offsets
    key_pos = key_block * width + offsets
    same_doc = query_seg[:, None] == key_seg[None, :]
    causal = key_pos[None, :] <= query_pos[:, None]
    return same_doc & causal & (key_block >= 0)


def tile_live(segments, query_block, key_block, width, offset):
    if offset == 0:
        return jnp.array(True)
    last_key = segments[jnp.maximum(key_block, 0) * width + width - 1]
    first_query = segments[query_block * width]
    return (key_block >= 0) & (last_key == first_query)


def tile_scores(query_tile, key_tile, allowed, score_scale):
    raw = (
        jnp.einsum("qhd,kd->hqk", query_tile, key_tile, preferred_element_type=jnp.float32)
        * score_scale
    )
    return jnp.where(allowed[None], raw, NEG_FILL)


def body(queries, key_states, value_states, out_grad, segments):
    devices = lax.axis_size("ctx")
    position = lax.axis_index("ctx")
    last_device = position == devices - 1
    width = queries.shape[2]
    head_dim = key_states.shape[3]
    head_count = queries.shape[3] // head_dim
    score_scale = head_dim ** (-0.5)
    query_blocks = [position, 2 * devices - 1 - position]
    key_blocks = []
    whole_keys, whole_values = (
        lax.all_gather(key_states, "head", axis=2, tiled=True),
        lax.all_gather(value_states, "head", axis=2, tiled=True),
    )
    lower = jnp.stack([whole_keys[0, 0], whole_values[0, 0]])
    upper = jnp.stack([whole_keys[0, 1], whole_values[0, 1]])
    for offset in range(REACH + 1):
        if offset > 0:
            lower, upper = advance_whole(lower, upper, last_device)
        key_blocks.append(jnp.stack([lower, upper]))
    query_tiles = [queries[0, half].reshape(width, head_count, head_dim) for half in range(2)]
    grad_tiles = [out_grad[0, half].reshape(width, head_count, head_dim) for half in range(2)]
    allowed_tiles = []
    live_tiles = []
    for offset in range(REACH + 1):
        allowed_tiles.append(
            [
                tile_allowed(segments, query_blocks[half], query_blocks[half] - offset, width)
                for half in range(2)
            ]
        )
        live_tiles.append(
            [
                tile_live(segments, query_blocks[half], query_blocks[half] - offset, width, offset)
                for half in range(2)
            ]
        )
    blank_scores = jnp.full((head_count, width, width), NEG_FILL, jnp.float32)
    score_tiles = [[blank_scores, blank_scores] for offset in range(REACH + 1)]
    log_totals = []
    for half in range(2):
        running_max = jnp.full((head_count, width), NEG_FILL, jnp.float32)
        running_sum = jnp.zeros((head_count, width), jnp.float32)
        for offset in range(REACH + 1):

            def first_pass(carried, offset=offset, half=half):
                old_max, old_sum, unused = carried
                scores = tile_scores(
                    query_tiles[half],
                    key_blocks[offset][half][0],
                    allowed_tiles[offset][half],
                    score_scale,
                )
                new_max = jnp.maximum(old_max, jnp.max(scores, axis=-1))
                new_sum = old_sum * jnp.exp(old_max - new_max) + jnp.sum(
                    jnp.exp(scores - new_max[:, :, None]), axis=-1
                )
                return (new_max, new_sum, scores)

            running_max, running_sum, kept_scores = first_pass(
                (running_max, running_sum, blank_scores)
            )
            score_tiles[offset][half] = kept_scores
        log_totals.append(running_max + jnp.log(running_sum))
    attended_tiles = []
    deltas = []
    for half in range(2):
        output_acc = jnp.zeros((width, head_count, head_dim), jnp.float32)
        for offset in range(REACH + 1):

            def second_pass(carried, offset=offset, half=half):
                weights = jnp.exp(score_tiles[offset][half] - log_totals[half][:, :, None]).astype(
                    jnp.bfloat16
                )
                return carried + jnp.einsum(
                    "hqk,kd->qhd",
                    weights,
                    key_blocks[offset][half][1],
                    preferred_element_type=jnp.float32,
                )

            output_acc = second_pass(output_acc)
        attended_tile = output_acc.astype(jnp.bfloat16)
        attended_tiles.append(attended_tile)
        deltas.append(
            jnp.einsum(
                "qhd,qhd->hq", grad_tiles[half], attended_tile, preferred_element_type=jnp.float32
            )
        )
    query_accs = [jnp.zeros((width, head_count, head_dim), jnp.float32) for half in range(2)]
    returned = None
    for offset in reversed(range(REACH + 1)):
        parts = []
        for half in range(2):
            key_tile = key_blocks[offset][half][0]
            value_tile = key_blocks[offset][half][1]

            def backward_tile(
                carried, half=half, key_tile=key_tile, value_tile=value_tile, offset=offset
            ):
                query_acc = carried[0]
                probs = jnp.exp(score_tiles[offset][half] - log_totals[half][:, :, None])
                weights = probs.astype(jnp.bfloat16)
                value_part = jnp.einsum(
                    "hqk,qhd->kd", weights, grad_tiles[half], preferred_element_type=jnp.float32
                )
                dot_grad = jnp.einsum(
                    "qhd,kd->hqk", grad_tiles[half], value_tile, preferred_element_type=jnp.float32
                )
                score_grad = (probs * (dot_grad - deltas[half][:, :, None])).astype(jnp.bfloat16)
                query_acc = (
                    query_acc
                    + jnp.einsum(
                        "hqk,kd->qhd", score_grad, key_tile, preferred_element_type=jnp.float32
                    )
                    * score_scale
                )
                key_part = (
                    jnp.einsum(
                        "hqk,qhd->kd",
                        score_grad,
                        query_tiles[half],
                        preferred_element_type=jnp.float32,
                    )
                    * score_scale
                )
                return (query_acc, key_part, value_part)

            empty_part = jnp.zeros((width, head_dim), jnp.float32)
            query_accs[half], key_part, value_part = backward_tile(
                (query_accs[half], empty_part, empty_part)
            )
            parts.append(jnp.stack([key_part, value_part]))
        contrib = jnp.stack(parts)
        if returned is not None:
            returned = retreat_whole(returned, last_device) + contrib
        else:
            returned = contrib
    returned = lax.psum_scatter(returned, "head", scatter_dimension=2, tiled=True)
    attended = jnp.stack([tile.reshape(width, head_count * head_dim) for tile in attended_tiles])[
        None
    ]
    query_grad = jnp.stack([acc.reshape(width, head_count * head_dim) for acc in query_accs])[
        None
    ].astype(jnp.bfloat16)
    key_grad = returned[:, 0][None].astype(jnp.bfloat16)
    value_grad = returned[:, 1][None].astype(jnp.bfloat16)
    return (attended, query_grad, key_grad, value_grad)


def solution(mesh):
    return jax.shard_map(
        body,
        mesh=mesh,
        in_specs=(
            P("ctx", None, None, "head"),
            P("ctx", None, "head", None),
            P("ctx", None, "head", None),
            P("ctx", None, None, "head"),
            P(),
        ),
        out_specs=(
            P("ctx", None, None, "head"),
            P("ctx", None, None, "head"),
            P("ctx", None, "head", None),
            P("ctx", None, "head", None),
        ),
        check_vma=False,
    )
```

profile of v0, /device:TPU:484, one launch (start us, length us, event | category | flops | bytes accessed | tf_op | source)
XLA Modules:
  0.0 433.3 jit_solution(10861266887282181746)
XLA Ops:
  0.6 0.8 copy.72
  1.4 47.1 %all_gather.6 = bf16[1,2,512,128]{3,1,0,2:T(2,128)(2,1)S(1)} all-gather(bf16[1,2,64,128]{3,1,0,2:T(2,128)(2,1)S(1)} %copy.72), channel_id=1, replica_groups=mesh['ctx'=64,'head'=8] {'head'}, dimensions={2}, use_global_device_ids=true | all-gather | bytes 294912 | tf_op jit(solution)/shard_map/all_gather | solution.py:66
  48.6 0.4 fusion.197
  49.1 0.6 copy-done.12
  49.7 46.8 %all_gather.7 = bf16[1,2,512,128]{3,1,0,2:T(2,128)(2,1)S(1)} all-gather(bf16[1,2,64,128]{3,1,0,2:T(2,128)(2,1)S(1)} %copy.74), channel_id=1, replica_groups=mesh['ctx'=64,'head'=8] {'head'}, dimensions={2}, use_global_device_ids=true | all-gather | bytes 294912 | tf_op jit(solution)/shard_map/all_gather | solution.py:67
  96.6 0.4 fusion.198
  97.1 0.7 pad_maximum_fusion.3
  97.8 1.9 collective-permute-start.3
  99.8 0.6 iota_add_fusion.4
  100.4 0.6 iota_add_fusion.5
  101.0 0.6 iota_add_fusion.6
  101.6 0.6 iota_add_fusion
  102.2 1.5 fusion.196
  103.7 0.5 fusion.202
  104.2 0.6 iota_add_fusion.1
  105.1 0.5 fusion.206
  105.7 1.0 broadcast_select_fusion.2
  106.7 2.4 collective-permute-start
  109.0 14.2 %collective-permute-start.4 = (bf16[2,512,128]{1,2,0:T(8,128)(2,1)S(1)}, bf16[2,512,128]{1,2,0:T(8,128)(2,1)}, u32[]{:S(2)}, u32[]{:S(2)}) collective-permute-start(bf16[2,512,128]{1,2,0:T(8,128)(2,1)S(1)} %get-tuple-element.40), channel_id=1, source_target_pairs={{8,0},{16,8},{24,16},{32,24},{40,32},{48,40},{56,48},{64,56},{72,6... | collective-permute-start | bytes 786440 | tf_op jit(solution)/shard_map/ppermute | solution.py:13
  123.2 0.6 iota_add_fusion.2
  123.8 1.3 dynamic-slice
  125.8 1.2 fusion.201
  127.0 1.4 collective-permute-done
  128.4 2.0 collective-permute-done.4
  130.4 1.0 broadcast_select_fusion.1
  131.4 14.7 %collective-permute-start.5 = (bf16[2,512,128]{1,2,0:T(8,128)(2,1)S(1)}, bf16[2,512,128]{1,2,0:T(8,128)(2,1)S(1)}, u32[]{:S(2)}, u32[]{:S(2)}) collective-permute-start(bf16[2,512,128]{1,2,0:T(8,128)(2,1)S(1)} %broadcast_select_fusion.1), channel_id=1, source_target_pairs={{8,0},{16,8},{24,16},{32,24},{40,32},{48,40},{56,48},{64,56},{72,6... | collective-permute-start | bytes 786440 | tf_op jit(solution)/shard_map/ppermute | solution.py:13
  146.1 1.9 collective-permute-start.1
  148.1 0.5 fusion.200
  148.8 0.5 fusion.205
  149.3 19.2 %collective-permute-done.1 = bf16[2,512,128]{1,2,0:T(8,128)(2,1)S(1)} collective-permute-done((bf16[2,512,128]{1,2,0:T(8,128)(2,1)S(1)}, bf16[2,512,128]{1,2,0:T(8,128)(2,1)S(1)}, u32[]{:S(2)}, u32[]{:S(2)}) %collective-permute-start.1) | collective-permute-done | bytes 262176 | tf_op jit(solution)/shard_map/ppermute | solution.py:13
  168.6 0.5 fusion.199
  170.5 0.6 copy-done
  172.0 1.0 convolution_bitcast_fusion.8
  173.0 0.4 fusion.66
  173.4 2.1 collective-permute-start.2
  175.5 0.5 fusion.204
  176.0 0.4 fusion.74
  176.4 16.6 %collective-permute-done.2 = bf16[2,512,128]{1,2,0:T(8,128)(2,1)S(1)} collective-permute-done((bf16[2,512,128]{1,2,0:T(8,128)(2,1)S(1)}, bf16[2,512,128]{1,2,0:T(8,128)(2,1)S(1)}, u32[]{:S(2)}, u32[]{:S(2)}) %collective-permute-start.2) | collective-permute-done | bytes 262176 | tf_op jit(solution)/shard_map/ppermute | solution.py:13
  193.0 0.5 fusion.203
  195.2 0.4 convolution_add_fusion.6
  195.5 0.4 convolution_add_fusion.5
  195.9 1.1 fusion.96
  198.3 1.0 convolution_bitcast_fusion.9
  201.1 0.6 copy-done.3
  203.8 1.9 collective-permute-start.6
  206.9 11.3 %collective-permute-done.6 = f32[2,512,128]{1,2,0:T(8,128)S(1)} collective-permute-done((f32[2,512,128]{1,2,0:T(8,128)S(1)}, f32[2,512,128]{1,2,0:T(8,128)S(1)}, u32[]{:S(2)}, u32[]{:S(2)}) %collective-permute-start.6) | collective-permute-done | bytes 524320 | tf_op jit(solution)/shard_map/ppermute | solution.py:13
  218.4 2.1 collective-permute-start.7
  221.0 24.6 %collective-permute-done.7 = f32[2,512,128]{1,2,0:T(8,128)S(1)} collective-permute-done((f32[2,512,128]{1,2,0:T(8,128)S(1)}, f32[2,512,128]{1,2,0:T(8,128)S(1)}, u32[]{:S(2)}, u32[]{:S(2)}) %collective-permute-start.7) | collective-permute-done | bytes 524320 | tf_op jit(solution)/shard_map/ppermute | solution.py:13
  245.8 1.9 collective-permute-start.8
  248.0 2.4 collective-permute-start.9
  250.7 3.7 collective-permute-done.8
  254.5 16.1 %collective-permute-done.9 = f32[2,512,128]{1,2,0:T(8,128)S(1)} collective-permute-done((f32[2,512,128]{1,2,0:T(8,128)S(1)}, f32[2,512,128]{1,2,0:T(8,128)S(1)}, u32[]{:S(2)}, u32[]{:S(2)}) %collective-permute-start.9) | collective-permute-done | bytes 524320 | tf_op jit(solution)/shard_map/ppermute | solution.py:13
  270.9 1.0 slice_bitcast_fusion
  271.9 1.9 collective-permute-start.10
  273.9 0.8 copy.104
  274.9 0.7 maximum_bitcast_fusion.6
  275.9 1.0 copy-done.11
  277.0 2.5 collective-permute-start.11
  279.9 6.1 %collective-permute-done.10 = f32[2,512,128]{1,2,0:T(8,128)} collective-permute-done((f32[2,512,128]{1,2,0:T(8,128)}, f32[2,512,128]{1,2,0:T(8,128)}, u32[]{:S(2)}, u32[]{:S(2)}) %collective-permute-start.10) | collective-permute-done | bytes 524320 | tf_op jit(solution)/shard_map/ppermute | solution.py:13
  285.9 1.1 select_bitcast_fusion
  287.1 18.4 %collective-permute-done.11 = f32[2,512,128]{1,2,0:T(8,128)S(1)} collective-permute-done((f32[2,512,128]{1,2,0:T(8,128)S(1)}, f32[2,512,128]{1,2,0:T(8,128)S(1)}, u32[]{:S(2)}, u32[]{:S(2)}) %collective-permute-start.11) | collective-permute-done | bytes 524320 | tf_op jit(solution)/shard_map/ppermute | solution.py:13
  305.7 0.7 copy.102
  306.5 126.1 %all-reduce.2 = bf16[2,2,512,128]{3,1,0,2:T(2,128)(2,1)S(1)} all-reduce(f32[2,2,512,128]{3,1,0,2:T(2,128)S(1)} %copy.102), channel_id=2, replica_groups=mesh['ctx'=64,'head'=8] {'head'}, use_global_device_ids=true, to_apply=%region_16.17.clone | all-reduce | flops 262144 | bytes 1572864
  432.6 0.6 slice_bitcast_fusion.40
  (119 shorter events, 13.8 us)
Async XLA Ops:
  48.9 0.8 copy-start.12
  97.1 6.6 %copy-start.1 = (bf16[1,2,512,128]{3,2,1,0:T(8,128)(2,1)S(1)}, bf16[1,2,512,128]{3,2,1,0:T(8,128)(2,1)}, u32[]{:S(2)}) copy-start(bf16[1,2,512,128]{3,2,1,0:T(8,128)(2,1)} %param.5) | copy-start | bytes 786436
  97.8 7.8 %collective-permute-start.3 = (bf16[2,512,128]{1,2,0:T(8,128)(2,1)}, bf16[2,512,128]{1,2,0:T(8,128)(2,1)}, u32[]{:S(2)}, u32[]{:S(2)}) collective-permute-start(bf16[2,512,128]{1,2,0:T(8,128)(2,1)} %pad_maximum_fusion.3), channel_id=1, source_target_pairs={{8,0},{16,8},{24,16},{32,24},{40,32},{48,40},{56,48},{64,56},{72,6... | collective-permute-start | bytes 786440 | tf_op jit(solution)/shard_map/ppermute | solution.py:13
  99.8 5.3 %copy-start.19 = (s32[512]{0:T(512)}, s32[512]{0:T(512)S(1)}, u32[]{:S(2)}) copy-start(s32[512]{0:T(512)S(1)} %iota_add_fusion.7) | copy-start | bytes 6148
  99.8 3.9 copy-start.23
  103.7 0.5 copy-start.14
  105.0 0.7 copy-start.6
  106.7 21.7 %collective-permute-start = (bf16[2,512,128]{1,2,0:T(8,128)(2,1)S(1)}, bf16[2,512,128]{1,2,0:T(8,128)(2,1)S(1)}, u32[]{:S(2)}, u32[]{:S(2)}) collective-permute-start(bf16[2,512,128]{1,2,0:T(8,128)(2,1)S(1)} %get-tuple-element.41), channel_id=1, source_target_pairs={{0,8},{8,16},{16,24},{24,32},{32,40},{40,48},{48,56},{56,64},{64,7... | collective-permute-start | bytes 786440 | tf_op jit(solution)/shard_map/ppermute | solution.py:13
  109.0 21.4 %collective-permute-start.4 = (bf16[2,512,128]{1,2,0:T(8,128)(2,1)S(1)}, bf16[2,512,128]{1,2,0:T(8,128)(2,1)}, u32[]{:S(2)}, u32[]{:S(2)}) collective-permute-start(bf16[2,512,128]{1,2,0:T(8,128)(2,1)S(1)} %get-tuple-element.40), channel_id=1, source_target_pairs={{8,0},{16,8},{24,16},{32,24},{40,32},{48,40},{56,48},{64,56},{72,6... | collective-permute-start | bytes 786440 | tf_op jit(solution)/shard_map/ppermute | solution.py:13
  127.0 21.1 %copy-start.15 = (s32[512]{0:T(512)S(1)}, s32[512]{0:T(512)}, u32[]{:S(2)}) copy-start(s32[512]{0:T(512)} %copy-done.14) | copy-start | bytes 6148
  127.0 21.1 %copy-start.18 = (s32[512]{0:T(512)S(1)}, s32[512]{0:T(512)}, u32[]{:S(2)}) copy-start(s32[512]{0:T(512)} %get-tuple-element.39) | copy-start | bytes 6148
  127.0 21.1 %copy-start.24 = (s32[512]{0:T(512)S(1)}, s32[512]{0:T(512)}, u32[]{:S(2)}) copy-start(s32[512]{0:T(512)} %copy-done.23) | copy-start | bytes 6148
  127.0 21.1 %copy-start.27 = (s32[512]{0:T(512)S(1)}, s32[512]{0:T(512)}, u32[]{:S(2)}) copy-start(s32[512]{0:T(512)} %iota_add_fusion.1) | copy-start | bytes 6148
  128.4 66.8 %copy-start.2 = (bf16[2,512,128]{1,2,0:T(8,128)(2,1)}, bf16[2,512,128]{1,2,0:T(8,128)(2,1)S(1)}, u32[]{:S(2)}) copy-start(bf16[2,512,128]{1,2,0:T(8,128)(2,1)S(1)} %collective-permute-done) | copy-start | bytes 786436
  131.4 37.1 %collective-permute-start.5 = (bf16[2,512,128]{1,2,0:T(8,128)(2,1)S(1)}, bf16[2,512,128]{1,2,0:T(8,128)(2,1)S(1)}, u32[]{:S(2)}, u32[]{:S(2)}) collective-permute-start(bf16[2,512,128]{1,2,0:T(8,128)(2,1)S(1)} %broadcast_select_fusion.1), channel_id=1, source_target_pairs={{8,0},{16,8},{24,16},{32,24},{40,32},{48,40},{56,48},{64,56},{72,6... | collective-permute-start | bytes 786440 | tf_op jit(solution)/shard_map/ppermute | solution.py:13
  146.1 22.4 %collective-permute-start.1 = (bf16[2,512,128]{1,2,0:T(8,128)(2,1)S(1)}, bf16[2,512,128]{1,2,0:T(8,128)(2,1)S(1)}, u32[]{:S(2)}, u32[]{:S(2)}) collective-permute-start(bf16[2,512,128]{1,2,0:T(8,128)(2,1)S(1)} %collective-permute-done), channel_id=1, source_target_pairs={{0,8},{8,16},{16,24},{24,32},{32,40},{40,48},{48,56},{56,64},{64,7... | collective-permute-start | bytes 786440 | tf_op jit(solution)/shard_map/ppermute | solution.py:13
  148.1 0.7 copy-start.17
  148.1 0.7 copy-start.20
  148.1 0.7 copy-start.26
  149.3 19.3 %copy-start.16 = (s32[512]{0:T(512)S(1)}, s32[512]{0:T(512)}, u32[]{:S(2)}) copy-start(s32[512]{0:T(512)} %get-tuple-element.38) | copy-start | bytes 6148
  149.3 19.3 %copy-start.25 = (s32[512]{0:T(512)S(1)}, s32[512]{0:T(512)}, u32[]{:S(2)}) copy-start(s32[512]{0:T(512)} %iota_add_fusion) | copy-start | bytes 6148
  170.1 1.0 copy-start
  173.0 2.5 copy-start.13
  173.0 2.5 copy-start.22
  173.4 19.6 %collective-permute-start.2 = (bf16[2,512,128]{1,2,0:T(8,128)(2,1)S(1)}, bf16[2,512,128]{1,2,0:T(8,128)(2,1)S(1)}, u32[]{:S(2)}, u32[]{:S(2)}) collective-permute-start(bf16[2,512,128]{1,2,0:T(8,128)(2,1)S(1)} %collective-permute-done.1), channel_id=1, source_target_pairs={{0,8},{8,16},{16,24},{24,32},{32,40},{40,48},{48,56},{56,64},{64,7... | collective-permute-start | bytes 786440 | tf_op jit(solution)/shard_map/ppermute | solution.py:13
  176.0 17.0 %copy-start.21 = (s32[512]{0:T(512)S(1)}, s32[512]{0:T(512)}, u32[]{:S(2)}) copy-start(s32[512]{0:T(512)} %iota_add_fusion.4) | copy-start | bytes 6148
  176.4 19.5 %copy-start.4 = (bf16[128,512]{0,1:T(8,128)(2,1)}, bf16[128,512]{0,1:T(8,128)(2,1)S(1)}, u32[]{:S(2)}) copy-start(bf16[128,512]{0,1:T(8,128)(2,1)S(1)} %fusion.74) | copy-start | bytes 393220
  200.8 1.0 copy-start.3
  203.8 14.5 %collective-permute-start.6 = (f32[2,512,128]{1,2,0:T(8,128)S(1)}, f32[2,512,128]{1,2,0:T(8,128)S(1)}, u32[]{:S(2)}, u32[]{:S(2)}) collective-permute-start(f32[2,512,128]{1,2,0:T(8,128)S(1)} %pad_maximum_fusion.1), channel_id=1, source_target_pairs={{8,0},{16,8},{24,16},{32,24},{40,32},{48,40},{56,48},{64,56},{72,6... | collective-permute-start | bytes 1572872 | tf_op jit(solution)/shard_map/ppermute | solution.py:13
  218.4 2.1 copy-start.7
  218.4 27.2 %collective-permute-start.7 = (f32[2,512,128]{1,2,0:T(8,128)S(1)}, f32[2,512,128]{1,2,0:T(8,128)S(1)}, u32[]{:S(2)}, u32[]{:S(2)}) collective-permute-start(f32[2,512,128]{1,2,0:T(8,128)S(1)} %get-tuple-element.29), channel_id=1, source_target_pairs={{0,8},{8,16},{16,24},{24,32},{32,40},{40,48},{48,56},{56,64},{64,7... | collective-permute-start | bytes 1572872 | tf_op jit(solution)/shard_map/ppermute | solution.py:13
  245.8 8.6 %collective-permute-start.8 = (f32[2,512,128]{1,2,0:T(8,128)S(1)}, f32[2,512,128]{1,2,0:T(8,128)S(1)}, u32[]{:S(2)}, u32[]{:S(2)}) collective-permute-start(f32[2,512,128]{1,2,0:T(8,128)S(1)} %get-tuple-element.26), channel_id=1, source_target_pairs={{8,0},{16,8},{24,16},{32,24},{40,32},{48,40},{56,48},{64,56},{72,6... | collective-permute-start | bytes 1572872 | tf_op jit(solution)/shard_map/ppermute | solution.py:13
  248.0 22.7 %collective-permute-start.9 = (f32[2,512,128]{1,2,0:T(8,128)S(1)}, f32[2,512,128]{1,2,0:T(8,128)S(1)}, u32[]{:S(2)}, u32[]{:S(2)}) collective-permute-start(f32[2,512,128]{1,2,0:T(8,128)S(1)} %get-tuple-element.27), channel_id=1, source_target_pairs={{0,8},{8,16},{16,24},{24,32},{32,40},{40,48},{48,56},{56,64},{64,7... | collective-permute-start | bytes 1572872 | tf_op jit(solution)/shard_map/ppermute | solution.py:13
  271.9 14.0 %collective-permute-start.10 = (f32[2,512,128]{1,2,0:T(8,128)}, f32[2,512,128]{1,2,0:T(8,128)}, u32[]{:S(2)}, u32[]{:S(2)}) collective-permute-start(f32[2,512,128]{1,2,0:T(8,128)} %get-tuple-element.24), channel_id=1, source_target_pairs={{8,0},{16,8},{24,16},{32,24},{40,32},{48,40},{56,48},{64,56},{72,6... | collective-permute-start | bytes 1572872 | tf_op jit(solution)/shard_map/ppermute | solution.py:13
  273.9 0.9 copy-start.5
  273.9 1.0 copy-start.10
  274.9 1.0 copy-start.9
  275.9 1.0 copy-start.11
  276.9 2.9 copy-start.8
  277.0 28.5 %collective-permute-start.11 = (f32[2,512,128]{1,2,0:T(8,128)S(1)}, f32[2,512,128]{1,2,0:T(8,128)S(1)}, u32[]{:S(2)}, u32[]{:S(2)}) collective-permute-start(f32[2,512,128]{1,2,0:T(8,128)S(1)} %copy-done.11), channel_id=1, source_target_pairs={{0,8},{8,16},{16,24},{24,32},{32,40},{40,48},{48,56},{56,64},{64,7... | collective-permute-start | bytes 1572872 | tf_op jit(solution)/shard_map/ppermute | solution.py:13
where the time goes:
time: 434 us; the launch traced here: 433 us
  blocking collectives  220 us (51%)
  waiting for transfers between devices  120 us (28%)
  starting transfers between devices  50 us (12%)
  matrix products  19.2 us (4%)
  local copies, waits for them, and re-layouts  11.8 us (3%)
  other arithmetic  10.4 us (2%)
    unnamed x1, blocking collectives  126 us
    ppermute x12, waiting for transfers between devices, shifted(): return lax.ppermute(array, axis, pairs)  120 us
    ppermute x12, starting transfers between devices, shifted(): return lax.ppermute(array, axis, pairs)  50 us
    all_gather x1, blocking collectives, body(): lax.all_gather(key_states, 'head', axis=2, tiled=True)  47.1 us
    all_gather x1, blocking collectives, body(): lax.all_gather(value_states, 'head', axis=2, tiled=True)  46.8 us
  transfers between devices with their start and end apart: 12, of which 10 were waited for; matrix products, arithmetic and copies ran while one was open for 4% of the time, Pallas kernels for 0%

commit v1 on v0

--- a/solution.py
+++ b/solution.py
@@ -63,7 +63,9 @@
     query_blocks = [position, 2 * devices - 1 - position]
     key_blocks = []
     whole_keys, whole_values = (
-        lax.all_gather(key_states, "head", axis=2, tiled=True),
+        jnp.concatenate(
+            lax.all_to_all(jnp.stack([key_states] * lax.axis_size("head")), "head", 0, 0), axis=2
+        ),
         lax.all_gather(value_states, "head", axis=2, tiled=True),
     )
     lower = jnp.stack([whole_keys[0, 0], whole_values[0, 0]])

time: 434 us -> 397 us (0.915)
  the two profiles are of different devices: /device:TPU:484 before, /device:TPU:6 now
where the time goes in v1:
time: 397 us; the launch traced here: 396 us
  blocking collectives  166 us (42%)
  waiting for transfers between devices  123 us (31%)
  starting transfers between devices  74.2 us (19%)
  matrix products  16.9 us (4%)
  local copies, waits for them, and re-layouts  9.67 us (2%)
  other arithmetic  4.25 us (1%)
    ppermute x12, waiting for transfers between devices, shifted(): return lax.ppermute(array, axis, pairs)  123 us
    unnamed x1, blocking collectives  115 us
    ppermute x12, starting transfers between devices, shifted(): return lax.ppermute(array, axis, pairs)  61.5 us
    all_gather x1, blocking collectives, body(): lax.all_gather(value_states, 'head', axis=2, tiled=True)  50.4 us
    all_to_all x1, starting transfers between devices, body(): lax.all_to_all(jnp.stack([key_states] * lax.axis_size('head')), 'head', 0...  12.7 us
  transfers between devices with their start and end apart: 13, of which 11 were waited for; matrix products, arithmetic and copies ran while one was open for 3% of the time, Pallas kernels for 0%

profile of v1, /device:TPU:6, one launch (start us, length us, event | category | flops | bytes accessed | tf_op | source)
XLA Modules:
  0.0 396.0 jit_solution(15401407162620241474)
XLA Ops:
  0.6 1.5 stack.153
  2.1 12.7 %all-to-all-start = ((bf16[8,1,2,64,128]{4,3,2,1,0:T(8,128)(2,1)}), bf16[8,1,2,64,128]{4,3,2,1,0:T(8,128)(2,1)S(1)}, u32[]{:S(2)}, u32[]{:S(2)}) async-start(bf16[8,1,2,64,128]{4,3,2,1,0:T(8,128)(2,1)} %stack.153), calls=%async_computation | async-start | bytes 524288 | tf_op jit(solution)/shard_map/all_to_all | solution.py:67
  14.9 50.4 %all_gather.3 = bf16[1,2,512,128]{3,1,0,2:T(2,128)(2,1)S(1)} all-gather(bf16[1,2,64,128]{3,1,0,2:T(2,128)(2,1)S(1)} %copy.104), channel_id=1, replica_groups=mesh['ctx'=64,'head'=8] {'head'}, dimensions={2}, use_global_device_ids=true | all-gather | bytes 294912 | tf_op jit(solution)/shard_map/all_gather | solution.py:69
  65.3 0.4 fusion.202
  65.9 1.0 fusion.200
  67.1 3.7 collective-permute-start.3
  71.0 1.3 dynamic-slice
  73.0 0.5 fusion.210
  73.5 3.2 collective-permute-done.3
  76.7 1.9 collective-permute-start
  78.6 15.5 %collective-permute-start.4 = (bf16[2,512,128]{1,2,0:T(8,128)(2,1)S(1)}, bf16[2,512,128]{1,2,0:T(8,128)(2,1)S(1)}, u32[]{:S(2)}, u32[]{:S(2)}) collective-permute-start(bf16[2,512,128]{1,2,0:T(8,128)(2,1)S(1)} %get-tuple-element.44), channel_id=1, source_target_pairs={{8,0},{16,8},{24,16},{32,24},{40,32},{48,40},{56,48},{64,56},{72,6... | collective-permute-start | bytes 786440 | tf_op jit(solution)/shard_map/ppermute | solution.py:13
  94.2 0.5 fusion.206
  94.6 0.5 fusion.205
  95.1 3.7 collective-permute-done
  98.8 0.4 collective-permute-done.4
  99.2 15.5 %collective-permute-start.5 = (bf16[2,512,128]{1,2,0:T(8,128)(2,1)S(1)}, bf16[2,512,128]{1,2,0:T(8,128)(2,1)S(1)}, u32[]{:S(2)}, u32[]{:S(2)}) collective-permute-start(bf16[2,512,128]{1,2,0:T(8,128)(2,1)S(1)} %broadcast_select_fusion.1), channel_id=1, source_target_pairs={{8,0},{16,8},{24,16},{32,24},{40,32},{48,40},{56,48},{64,56},{72,6... | collective-permute-start | bytes 786440 | tf_op jit(solution)/shard_map/ppermute | solution.py:13
  114.7 1.9 collective-permute-start.1
  116.7 0.5 fusion.204
  117.2 0.5 fusion.209
  117.7 18.9 %collective-permute-done.1 = bf16[2,512,128]{1,2,0:T(8,128)(2,1)S(1)} collective-permute-done((bf16[2,512,128]{1,2,0:T(8,128)(2,1)S(1)}, bf16[2,512,128]{1,2,0:T(8,128)(2,1)S(1)}, u32[]{:S(2)}, u32[]{:S(2)}) %collective-permute-start.1) | collective-permute-done | bytes 262176 | tf_op jit(solution)/shard_map/ppermute | solution.py:13
  136.6 0.5 fusion.203
  137.7 0.3 convolution_bitcast_fusion.16
  138.1 0.4 fusion.110
  138.5 0.6 copy-done
  139.4 0.3 convolution_bitcast_fusion.15
  140.3 0.4 fusion.66
  140.7 2.1 collective-permute-start.2
  142.8 0.5 fusion.208
  143.3 0.4 fusion.74
  143.7 17.0 %collective-permute-done.2 = bf16[2,512,128]{1,2,0:T(8,128)(2,1)S(1)} collective-permute-done((bf16[2,512,128]{1,2,0:T(8,128)(2,1)S(1)}, bf16[2,512,128]{1,2,0:T(8,128)(2,1)S(1)}, u32[]{:S(2)}, u32[]{:S(2)}) %collective-permute-start.2) | collective-permute-done | bytes 262176 | tf_op jit(solution)/shard_map/ppermute | solution.py:13
  160.7 0.5 fusion.207
  161.9 0.3 convolution_bitcast_fusion.17
  162.8 0.3 convolution_bitcast_fusion.14
  163.2 0.4 convolution_add_fusion.6
  163.5 0.4 convolution_add_fusion.5
  163.9 1.0 fusion.96
  165.3 0.3 fusion.52
  165.6 0.3 fusion.54
  165.9 0.3 convolution_bitcast_fusion.9
  166.3 0.3 fusion.55
  167.1 0.3 fusion.60
  167.7 0.3 fusion.51
  168.0 0.3 fusion.50
  168.7 0.3 fusion.49
  169.3 0.3 fusion.48
  170.0 1.9 collective-permute-start.6
  173.2 8.3 %collective-permute-done.6 = f32[2,512,128]{1,2,0:T(8,128)S(1)} collective-permute-done((f32[2,512,128]{1,2,0:T(8,128)S(1)}, f32[2,512,128]{1,2,0:T(8,128)S(1)}, u32[]{:S(2)}, u32[]{:S(2)}) %collective-permute-start.6) | collective-permute-done | bytes 524320 | tf_op jit(solution)/shard_map/ppermute | solution.py:13
  181.6 1.9 collective-permute-start.7
  184.1 28.7 %collective-permute-done.7 = f32[2,512,128]{1,2,0:T(8,128)S(1)} collective-permute-done((f32[2,512,128]{1,2,0:T(8,128)S(1)}, f32[2,512,128]{1,2,0:T(8,128)S(1)}, u32[]{:S(2)}, u32[]{:S(2)}) %collective-permute-start.7) | collective-permute-done | bytes 524320 | tf_op jit(solution)/shard_map/ppermute | solution.py:13
  213.1 1.9 collective-permute-start.8
  215.2 2.4 collective-permute-start.9
  218.0 3.9 collective-permute-done.8
  221.9 18.9 %collective-permute-done.9 = f32[2,512,128]{1,2,0:T(8,128)S(1)} collective-permute-done((f32[2,512,128]{1,2,0:T(8,128)S(1)}, f32[2,512,128]{1,2,0:T(8,128)S(1)}, u32[]{:S(2)}, u32[]{:S(2)}) %collective-permute-start.9) | collective-permute-done | bytes 524320 | tf_op jit(solution)/shard_map/ppermute | solution.py:13
  241.0 1.1 slice_bitcast_fusion
  242.1 10.7 %collective-permute-start.10 = (f32[2,512,128]{1,2,0:T(8,128)}, f32[2,512,128]{1,2,0:T(8,128)S(1)}, u32[]{:S(2)}, u32[]{:S(2)}) collective-permute-start(f32[2,512,128]{1,2,0:T(8,128)} %get-tuple-element.28), channel_id=1, source_target_pairs={{8,0},{16,8},{24,16},{32,24},{40,32},{48,40},{56,48},{64,56},{72,6... | collective-permute-start | bytes 1572872 | tf_op jit(solution)/shard_map/ppermute | solution.py:13
  252.9 0.8 copy.134
  253.7 1.6 maximum_bitcast_fusion.6
  255.4 1.0 copy-done.2
  256.4 1.9 collective-permute-start.11
  258.7 1.2 collective-permute-done.10
  259.9 18.9 %collective-permute-done.11 = f32[2,512,128]{1,2,0:T(8,128)S(1)} collective-permute-done((f32[2,512,128]{1,2,0:T(8,128)S(1)}, f32[2,512,128]{1,2,0:T(8,128)S(1)}, u32[]{:S(2)}, u32[]{:S(2)}) %collective-permute-start.11) | collective-permute-done | bytes 524320 | tf_op jit(solution)/shard_map/ppermute | solution.py:13
  279.1 0.7 copy.132
  279.8 115.5 %all-reduce.2 = bf16[2,2,512,128]{3,1,0,2:T(2,128)(2,1)S(1)} all-reduce(f32[2,2,512,128]{3,1,0,2:T(2,128)S(1)} %copy.132), channel_id=2, replica_groups=mesh['ctx'=64,'head'=8] {'head'}, use_global_device_ids=true, to_apply=%region_16.17.clone | all-reduce | flops 262144 | bytes 1572864
  395.4 0.6 slice_bitcast_fusion.40
  (73 shorter events, 9.3 us)
Async XLA Ops:
  2.1 12.7 %copy-start.3 = (bf16[1,2,64,128]{3,2,1,0:T(8,128)(2,1)S(1)}, bf16[1,2,64,128]{3,2,1,0:T(8,128)(2,1)}, u32[]{:S(2)}) copy-start(bf16[1,2,64,128]{3,2,1,0:T(8,128)(2,1)} %param.7) | copy-start | bytes 98308
  2.1 64.7 %all-to-all-start = ((bf16[8,1,2,64,128]{4,3,2,1,0:T(8,128)(2,1)}), bf16[8,1,2,64,128]{4,3,2,1,0:T(8,128)(2,1)S(1)}, u32[]{:S(2)}, u32[]{:S(2)}) async-start(bf16[8,1,2,64,128]{4,3,2,1,0:T(8,128)(2,1)} %stack.153), calls=%async_computation | async-start | bytes 524288 | tf_op jit(solution)/shard_map/all_to_all | solution.py:67
  67.1 9.6 %collective-permute-start.3 = (bf16[2,512,128]{1,2,0:T(8,128)(2,1)S(1)}, bf16[2,512,128]{1,2,0:T(8,128)(2,1)S(1)}, u32[]{:S(2)}, u32[]{:S(2)}) collective-permute-start(bf16[2,512,128]{1,2,0:T(8,128)(2,1)S(1)} %pad_maximum_fusion.3), channel_id=1, source_target_pairs={{8,0},{16,8},{24,16},{32,24},{40,32},{48,40},{56,48},{64,56},{72,6... | collective-permute-start | bytes 786440 | tf_op jit(solution)/shard_map/ppermute | solution.py:13
  70.8 2.2 copy-start.1
  76.7 22.1 %collective-permute-start = (bf16[2,512,128]{1,2,0:T(8,128)(2,1)S(1)}, bf16[2,512,128]{1,2,0:T(8,128)(2,1)S(1)}, u32[]{:S(2)}, u32[]{:S(2)}) collective-permute-start(bf16[2,512,128]{1,2,0:T(8,128)(2,1)S(1)} %get-tuple-element.45), channel_id=1, source_target_pairs={{0,8},{8,16},{16,24},{24,32},{32,40},{40,48},{48,56},{56,64},{64,7... | collective-permute-start | bytes 786440 | tf_op jit(solution)/shard_map/ppermute | solution.py:13
  78.6 20.5 %collective-permute-start.4 = (bf16[2,512,128]{1,2,0:T(8,128)(2,1)S(1)}, bf16[2,512,128]{1,2,0:T(8,128)(2,1)S(1)}, u32[]{:S(2)}, u32[]{:S(2)}) collective-permute-start(bf16[2,512,128]{1,2,0:T(8,128)(2,1)S(1)} %get-tuple-element.44), channel_id=1, source_target_pairs={{8,0},{16,8},{24,16},{32,24},{40,32},{48,40},{56,48},{64,56},{72,6... | collective-permute-start | bytes 786440 | tf_op jit(solution)/shard_map/ppermute | solution.py:13
  99.2 37.4 %collective-permute-start.5 = (bf16[2,512,128]{1,2,0:T(8,128)(2,1)S(1)}, bf16[2,512,128]{1,2,0:T(8,128)(2,1)S(1)}, u32[]{:S(2)}, u32[]{:S(2)}) collective-permute-start(bf16[2,512,128]{1,2,0:T(8,128)(2,1)S(1)} %broadcast_select_fusion.1), channel_id=1, source_target_pairs={{8,0},{16,8},{24,16},{32,24},{40,32},{48,40},{56,48},{64,56},{72,6... | collective-permute-start | bytes 786440 | tf_op jit(solution)/shard_map/ppermute | solution.py:13
  114.7 21.8 %collective-permute-start.1 = (bf16[2,512,128]{1,2,0:T(8,128)(2,1)S(1)}, bf16[2,512,128]{1,2,0:T(8,128)(2,1)S(1)}, u32[]{:S(2)}, u32[]{:S(2)}) collective-permute-start(bf16[2,512,128]{1,2,0:T(8,128)(2,1)S(1)} %collective-permute-done), channel_id=1, source_target_pairs={{0,8},{8,16},{16,24},{24,32},{32,40},{40,48},{48,56},{56,64},{64,7... | collective-permute-start | bytes 786440 | tf_op jit(solution)/shard_map/ppermute | solution.py:13
  138.1 1.0 copy-start
  140.7 20.0 %collective-permute-start.2 = (bf16[2,512,128]{1,2,0:T(8,128)(2,1)S(1)}, bf16[2,512,128]{1,2,0:T(8,128)(2,1)S(1)}, u32[]{:S(2)}, u32[]{:S(2)}) collective-permute-start(bf16[2,512,128]{1,2,0:T(8,128)(2,1)S(1)} %collective-permute-done.1), channel_id=1, source_target_pairs={{0,8},{8,16},{16,24},{24,32},{32,40},{40,48},{48,56},{56,64},{64,7... | collective-permute-start | bytes 786440 | tf_op jit(solution)/shard_map/ppermute | solution.py:13
  170.0 11.5 %collective-permute-start.6 = (f32[2,512,128]{1,2,0:T(8,128)S(1)}, f32[2,512,128]{1,2,0:T(8,128)S(1)}, u32[]{:S(2)}, u32[]{:S(2)}) collective-permute-start(f32[2,512,128]{1,2,0:T(8,128)S(1)} %pad_maximum_fusion.1), channel_id=1, source_target_pairs={{8,0},{16,8},{24,16},{32,24},{40,32},{48,40},{56,48},{64,56},{72,6... | collective-permute-start | bytes 1572872 | tf_op jit(solution)/shard_map/ppermute | solution.py:13
  181.6 31.2 %collective-permute-start.7 = (f32[2,512,128]{1,2,0:T(8,128)S(1)}, f32[2,512,128]{1,2,0:T(8,128)S(1)}, u32[]{:S(2)}, u32[]{:S(2)}) collective-permute-start(f32[2,512,128]{1,2,0:T(8,128)S(1)} %get-tuple-element.33), channel_id=1, source_target_pairs={{0,8},{8,16},{16,24},{24,32},{32,40},{40,48},{48,56},{56,64},{64,7... | collective-permute-start | bytes 1572872 | tf_op jit(solution)/shard_map/ppermute | solution.py:13
  213.1 8.8 %collective-permute-start.8 = (f32[2,512,128]{1,2,0:T(8,128)S(1)}, f32[2,512,128]{1,2,0:T(8,128)S(1)}, u32[]{:S(2)}, u32[]{:S(2)}) collective-permute-start(f32[2,512,128]{1,2,0:T(8,128)S(1)} %get-tuple-element.30), channel_id=1, source_target_pairs={{8,0},{16,8},{24,16},{32,24},{40,32},{48,40},{56,48},{64,56},{72,6... | collective-permute-start | bytes 1572872 | tf_op jit(solution)/shard_map/ppermute | solution.py:13
  215.2 25.6 %collective-permute-start.9 = (f32[2,512,128]{1,2,0:T(8,128)S(1)}, f32[2,512,128]{1,2,0:T(8,128)S(1)}, u32[]{:S(2)}, u32[]{:S(2)}) collective-permute-start(f32[2,512,128]{1,2,0:T(8,128)S(1)} %get-tuple-element.31), channel_id=1, source_target_pairs={{0,8},{8,16},{16,24},{24,32},{32,40},{40,48},{48,56},{56,64},{64,7... | collective-permute-start | bytes 1572872 | tf_op jit(solution)/shard_map/ppermute | solution.py:13
  242.1 17.7 %collective-permute-start.10 = (f32[2,512,128]{1,2,0:T(8,128)}, f32[2,512,128]{1,2,0:T(8,128)S(1)}, u32[]{:S(2)}, u32[]{:S(2)}) collective-permute-start(f32[2,512,128]{1,2,0:T(8,128)} %get-tuple-element.28), channel_id=1, source_target_pairs={{8,0},{16,8},{24,16},{32,24},{40,32},{48,40},{56,48},{64,56},{72,6... | collective-permute-start | bytes 1572872 | tf_op jit(solution)/shard_map/ppermute | solution.py:13
  255.4 1.0 copy-start.2
  256.4 22.5 %collective-permute-start.11 = (f32[2,512,128]{1,2,0:T(8,128)S(1)}, f32[2,512,128]{1,2,0:T(8,128)S(1)}, u32[]{:S(2)}, u32[]{:S(2)}) collective-permute-start(f32[2,512,128]{1,2,0:T(8,128)S(1)} %copy-done.2), channel_id=1, source_target_pairs={{0,8},{8,16},{16,24},{24,32},{32,40},{40,48},{48,56},{56,64},{64,7... | collective-permute-start | bytes 1572872 | tf_op jit(solution)/shard_map/ppermute | solution.py:13
